TPU v7x, 32 devices: a whole 2x2x4 slice. The times are simulated.
32 devices in a mesh: seq: 8 (over y, x, core), ch: 4 (over z).
Axes of the slice: x: 2, y: 2, z: 4, core: 2. Of those that a mesh axis runs over, the one named last changes fastest.
Arguments:
- token_ids: int32 [8192], P('seq'), may hold values from 0 to 511
- embedding: bfloat16 [4096, 512], P('ch'), may hold values from -26 to 26
- projected: bfloat16 [3, 4096, 512], P(None, 'ch'), may hold values from -6 to 6
- short_taps: float32 [7, 3, 4096], P(None, None, 'ch'), may hold values from -2 to 2
- long_filter: bfloat16 [4096, 8192], P('ch', 'seq'), may hold values from -1.6 to 1.6
- skip_gain: float32 [4096], P('ch'), may hold values from -3 to 3
Outputs:
- mixed: bfloat16 [4096, 8192], P('ch', 'seq')
All inputs are finite; a program needn't handle non-finite values.
Results may differ from a plain program's by a relative error of at most 0.0075.
Values may be sent and summed in bfloat16 or wider, within the bound.
A program may use at most 192 MiB of HBM per device.

v0:
```python
import functools
import math

import jax
import jax.numpy as jnp
import numpy as np
from jax import lax
from jax.experimental import pallas as pl
from jax.experimental.pallas import tpu as pltpu
from jax.sharding import PartitionSpec as P

MIXER_CHANNELS = 4096
EPSILON = 1e-06
LANES = 128
GROUP = 16
BATCH = 8
HISTORY = 8
VMEM_LIMIT = 56 * 1024 * 1024
MESH = pl.DeviceIdType.MESH


def transform_tables(length):
    coarse = length // LANES
    k1 = np.arange(coarse)[:, None] + 0.25
    phi = 2.0 * np.pi * k1 * np.arange(coarse)[None, :] / coarse
    first = np.concatenate([np.cos(phi), -np.sin(phi)], axis=0)
    psi = 2.0 * np.pi * k1 * np.arange(LANES)[None, :] / length
    fine = np.arange(LANES)
    chi = 2.0 * np.pi * (fine[:, None] * fine[None, :] % LANES) / LANES
    c, s = np.cos(chi), np.sin(chi)
    second = np.block([[c, -s], [s, c]])
    second_inv = np.block([[c, s], [-s, c]])
    bf = jnp.bfloat16
    return (
        jnp.asarray(first, bf),
        jnp.asarray(first.T / length, bf),
        jnp.asarray(np.cos(psi), jnp.float32),
        jnp.asarray(np.sin(psi), jnp.float32),
        jnp.asarray(second, bf),
        jnp.asarray(second_inv, bf),
    )


def mixer_kernel(
    seq_count, ch_count,
    ids_ref, squares_ref, proj_ref, taps_ref, filter_ref, skip_ref,
    t1_ref, t1i_ref, c_ref, s_ref, w2_ref, w2i_ref,
    out_ref,
    ids_all, squares_all, table, feats, first, zs, filt, hs, ys, send,
    ids_send, ids_recv, sq_send, sq_recv, filt_send, filt_recv, filt_own, out_send, out_recv, out_own,
):
    me, ch = lax.axis_index("seq"), lax.axis_index("ch")
    step, steps = pl.program_id(0), pl.num_programs(0)
    groups, blocks, rows, tokens = filt.shape
    group = groups * rows
    per = tokens // LANES
    coarse = blocks * per
    vocab = table.shape[0]
    width = table.shape[1] // 3
    taps = taps_ref.shape[0]
    f32, bf = jnp.float32, jnp.bfloat16

    def rows_of(g):
        return pl.ds(pl.multiple_of(g * rows, rows), rows)

    def remote(src, dst, sent, received, device):
        return pltpu.make_async_remote_copy(
            src_ref=src, dst_ref=dst, send_sem=sent, recv_sem=received,
            device_id=device, device_id_type=MESH,
        )

    def along_seq(d):
        return (lax.rem(me + d, seq_count), ch)

    def along_ch(d):
        return (me, lax.rem(ch + d, ch_count))

    def filter_to(g, d):
        peer = along_seq(d)
        return remote(
            filter_ref.at[peer[0], rows_of(g), :], filt.at[g, me],
            filt_send.at[g, d], filt_recv.at[g, d], peer,
        )

    def filter_kept(g):
        return pltpu.make_async_copy(
            filter_ref.at[me, rows_of(g), :], filt.at[g, me], filt_own.at[g]
        )

    def result_to(g, d):
        peer = along_seq(d)
        return remote(
            send.at[g, peer[0]], out_ref.at[me, rows_of(g), :],
            out_send.at[g, d], out_recv.at[g, d], peer,
        )

    def result_kept(g):
        return pltpu.make_async_copy(send.at[g, me], out_ref.at[me, rows_of(g), :], out_own.at[g])

    @pl.when(step == 0)
    def _():
        barrier = pltpu.get_barrier_semaphore()
        for d in range(1, seq_count):
            pl.semaphore_signal(barrier, inc=1, device_id=along_seq(d), device_id_type=MESH)
        for d in range(1, ch_count):
            pl.semaphore_signal(barrier, inc=1, device_id=along_ch(d), device_id_type=MESH)
        pl.semaphore_wait(barrier, seq_count + ch_count - 2)
        small = [
            remote(squares_ref, squares_all.at[ch], sq_send.at[d], sq_recv.at[d], along_ch(d))
            for d in range(1, ch_count)
        ] + [
            remote(ids_ref, ids_all.at[me], ids_send.at[d], ids_recv.at[d], along_seq(d))
            for d in range(1, seq_count)
        ]
        for copy in small:
            copy.start()

        @pl.loop(0, groups)
        def _(g):
            @pl.loop(1, blocks)
            def _(d):
                filter_to(g, d).start()

            filter_kept(g).start()

        ids_all[me] = ids_ref[...]
        squares_all[ch] = squares_ref[...]
        feats[:HISTORY] = jnp.zeros((HISTORY, 3 * width), f32)
        for copy in small:
            copy.wait()
        total = squares_all[0]
        for other in range(1, ch_count):
            total = total + squares_all[other]
        scale = 1.0 / jnp.sqrt(total / MIXER_CHANNELS + EPSILON)
        for v in range(vocab // LANES):
            at = slice(v * LANES, (v + 1) * LANES)
            column = jnp.broadcast_to(scale[:, at], (LANES, LANES)).T[:, :1]
            table[at] = (proj_ref[at].astype(f32) * column).astype(bf)

    @pl.when(step < blocks)
    def _():
        @pl.when(step > 0)
        def _():
            feats[:HISTORY] = feats[tokens:]

        lane = lax.broadcasted_iota(jnp.int32, (LANES, vocab), 1).astype(f32)
        for i in range(per):
            ids = ids_all[step, :, i * LANES : (i + 1) * LANES].astype(f32)
            column = jnp.broadcast_to(ids, (LANES, LANES)).T[:, :1]
            onehot = (lane == column).astype(bf)
            feats[HISTORY + i * LANES : HISTORY + (i + 1) * LANES] = jnp.dot(
                onehot, table[...], preferred_element_type=f32
            )

        def stream(j, start):
            cols = slice(j * width, (j + 1) * width)
            acc = taps_ref[0:1, cols] * feats[start : start + LANES, cols]
            for k in range(1, taps):
                acc = acc + taps_ref[k : k + 1, cols] * feats[start - k : start - k + LANES, cols]
            return acc

        for i in range(per):
            start = HISTORY + i * LANES
            gated = (stream(1, start) * stream(2, start)).astype(bf).astype(f32)
            zs[pl.ds(step * per + i, group, stride=coarse), :] = gated.T[:group]
            first[step, :, i * LANES : (i + 1) * LANES] = stream(0, start).T[:group]

    @pl.when(step >= blocks)
    def _():
        g = step - blocks
        filter_kept(g).wait()

        @pl.loop(1, blocks)
        def _(d):
            filter_to(g, d).wait()

        for s in range(blocks):
            for q in range(per):
                cols = slice(q * LANES, (q + 1) * LANES)
                hs[pl.ds(s * per + q, rows, stride=coarse), :] = filt[g, s, :, cols].astype(f32)

        cos, sin = c_ref[...], s_ref[...]

        @pl.loop(0, rows // BATCH)
        def _(turn):
            base = pl.multiple_of(turn * (BATCH * coarse), BATCH * coarse)
            zbase = pl.multiple_of((g * rows + turn * BATCH) * coarse, BATCH * coarse)
            parts = []
            for i in range(BATCH):
                z = zs[pl.ds(zbase + i * coarse, coarse), :]
                h = hs[pl.ds(base + i * coarse, coarse), :]
                both = jnp.concatenate([z, h], axis=1).astype(bf)
                spread = jnp.dot(t1_ref[...], both, preferred_element_type=f32)
                for side in range(2):
                    cols = slice(side * LANES, (side + 1) * LANES)
                    re, im = spread[:coarse, cols], spread[coarse:, cols]
                    parts.append(
                        jnp.concatenate([re * cos + im * sin, im * cos - re * sin], axis=1).astype(bf)
                    )
            spectra = jnp.dot(
                jnp.concatenate(parts, axis=0), w2_ref[...], preferred_element_type=f32
            )
            parts = []
            for i in range(BATCH):
                z = spectra[2 * i * coarse : (2 * i + 1) * coarse]
                h = spectra[(2 * i + 1) * coarse : (2 * i + 2) * coarse]
                zr, zi, hr, hi = z[:, :LANES], z[:, LANES:], h[:, :LANES], h[:, LANES:]
                parts.append(
                    jnp.concatenate([zr * hr - zi * hi, zr * hi + zi * hr], axis=1).astype(bf)
                )
            back = jnp.dot(jnp.concatenate(parts, axis=0), w2i_ref[...], preferred_element_type=f32)
            for i in range(0, BATCH, 2):
                cols = []
                for o in range(2):
                    p = back[(i + o) * coarse : (i + o + 1) * coarse]
                    re, im = p[:, :LANES], p[:, LANES:]
                    cols.append(jnp.concatenate([re * cos - im * sin, im * cos + re * sin], axis=0))
                res = jnp.dot(
                    t1i_ref[...], jnp.concatenate(cols, axis=1).astype(bf), preferred_element_type=f32
                )
                for o in range(2):
                    skip = skip_ref[g * rows + turn * BATCH + i + o]
                    z = zs[pl.ds(zbase + (i + o) * coarse, coarse), :]
                    ys[pl.ds(base + (i + o) * coarse, coarse), :] = (
                        res[:, o * LANES : (o + 1) * LANES] + skip * z
                    )

        for s in range(blocks):
            for q in range(per):
                cols = slice(q * LANES, (q + 1) * LANES)
                long_out = ys[pl.ds(s * per + q, rows, stride=coarse), :].astype(bf)
                send[g, s, :, cols] = (first[s, rows_of(g), cols] * long_out.astype(f32)).astype(bf)

        @pl.loop(1, blocks)
        def _(d):
            result_to(g, d).start()

        result_kept(g).start()

    @pl.when(step == steps - 1)
    def _():
        @pl.loop(0, groups)
        def _(g):
            result_kept(g).wait()

            @pl.loop(1, blocks)
            def _(d):
                result_to(g, d).wait()


def mix(ids, squares, proj, taps_rows, filt, skip, ch_count):
    blocks, group, tokens = filt.shape
    length = blocks * tokens
    coarse = length // LANES
    groups = group // GROUP
    vocab, wide = proj.shape
    tables = transform_tables(length)
    f32, bf = jnp.float32, jnp.bfloat16
    dma, vmem = pltpu.SemaphoreType.DMA, pltpu.VMEM
    whole = lambda t: pl.BlockSpec(t.shape, lambda i: (0, 0))
    anywhere = pl.BlockSpec(memory_space=pl.ANY)
    return pl.pallas_call(
        functools.partial(mixer_kernel, blocks, ch_count),
        grid=(blocks + groups,),
        out_shape=jax.ShapeDtypeStruct((blocks, group, tokens), bf),
        in_specs=[whole(ids), whole(squares), whole(proj), whole(taps_rows), anywhere]
        + [pl.BlockSpec(memory_space=pltpu.SMEM)]
        + [whole(t) for t in tables],
        out_specs=anywhere,
        scratch_shapes=[
            vmem((blocks, 1, tokens), jnp.int32),
            vmem((ch_count, 1, vocab), f32),
            vmem((vocab, wide), bf),
            vmem((HISTORY + tokens, wide), f32),
            vmem((blocks, group, tokens), f32),
            vmem((group * coarse, LANES), f32),
            vmem((groups, blocks, GROUP, tokens), bf),
            vmem((GROUP * coarse, LANES), f32),
            vmem((GROUP * coarse, LANES), f32),
            vmem((groups, blocks, GROUP, tokens), bf),
            dma((blocks,)),
            dma((blocks,)),
            dma((ch_count,)),
            dma((ch_count,)),
            dma((groups, blocks)),
            dma((groups, blocks)),
            dma((groups,)),
            dma((groups, blocks)),
            dma((groups, blocks)),
            dma((groups,)),
        ],
        compiler_params=pltpu.CompilerParams(
            vmem_limit_bytes=VMEM_LIMIT, collective_id=0, has_side_effects=True
        ),
        cost_estimate=pl.CostEstimate(
            flops=2 * group * coarse * 4 * 256 * 256 + 2 * wide * vocab * length,
            bytes_accessed=group * length * 4,
            transcendentals=0,
        ),
    )(ids, squares, proj, taps_rows, filt, skip, *tables)


def shards(token_ids, embedding, projected, short_taps, long_filter, skip_gain):
    seq_count = lax.axis_size("seq")
    seq_index = lax.axis_index("seq")
    local_ch, vocab = embedding.shape
    tokens = token_ids.shape[0]
    taps = short_taps.shape[0]
    group = local_ch // seq_count
    start = seq_index * group

    values = embedding.astype(jnp.float32)
    squares = jnp.sum(values * values, axis=0)[None, :]
    proj = lax.dynamic_slice_in_dim(projected, start, group, axis=1)
    taps_rows = lax.dynamic_slice_in_dim(short_taps, start, group, axis=2)
    skip = lax.dynamic_slice_in_dim(skip_gain, start, group)
    width = -(-group // LANES) * LANES
    if width != group:
        proj = jnp.pad(proj, ((0, 0), (0, width - group), (0, 0)))
        taps_rows = jnp.pad(taps_rows, ((0, 0), (0, 0), (0, width - group)))
    mixed = mix(
        token_ids[None, :],
        squares,
        proj.reshape(3 * width, vocab).T,
        taps_rows.reshape(taps, 3 * width),
        long_filter.reshape(seq_count, group, tokens),
        skip,
        lax.axis_size("ch"),
    )
    return mixed.reshape(local_ch, tokens)


def solution(mesh):
    placed = (
        P("seq"),
        P("ch", None),
        P(None, "ch", None),
        P(None, None, "ch"),
        P("ch", "seq"),
        P("ch"),
    )
    return jax.shard_map(
        shards, mesh=mesh, in_specs=placed, out_specs=P("ch", "seq"), check_vma=False
    )
```

profile of v0, /device:TPU:0, one launch (start us, length us, event | category | flops | bytes accessed | tf_op | source)
XLA Modules:
  0.0 68.1 jit_solution(10431222270802046504)
XLA Ops:
  0.0 0.0 copy-start
  0.0 1.4 %dynamic_slice.11.skip_ref = f32[128]{0:T(128)} dynamic-slice(f32[1024]{0:T(1024)} %param.17, s32[]{:T(128)S(6)} %select_n.2), dynamic_slice_sizes={128} | dynamic-slice | bytes 1028 | tf_op jit(solution)/shard_map/dynamic_slice | solution.py:316
  1.4 2.1 %multiply_reduce_fusion = f32[512]{0:T(512)} fusion(bf16[1024,512]{1,0:T(8,128)(2,1)} %param.13), kind=kLoop, calls=%fused_computation | loop fusion | flops 1572352 | bytes 1050624 | tf_op jit(solution)/shard_map/reduce_sum | solution.py:313
  3.5 1.3 %dynamic-slice_bitcast_fusion.taps_ref = f32[7,384]{1,0:T(8,128)} fusion(f32[7,3,1024]{2,0,1:T(8,128)} %param.15, s32[]{:T(128)S(6)} %select_n.2), kind=kLoop, calls=%fused_computation.1 | loop fusion | bytes 21508 | tf_op jit(solution)/shard_map/reshape | solution.py:325
  4.8 0.0 copy-done
  4.8 0.9 %copy.14 = bf16[384,512]{0,1:T(8,128)(2,1)} copy(bf16[384,512]{1,0:T(8,128)(2,1)S(1)} %bitcast.9) | data formatting | bytes 786432 | tf_op jit(solution)/shard_map/reshape | solution.py:324
  5.8 59.2 %shard_map.118 = bf16[8,128,1024]{2,1,0:T(8,128)(2,1)} custom-call(s32[1,1024]{1,0:T(1,128)} %bitcast.13, f32[1,512]{1,0:T(1,128)} %bitcast.11, bf16[512,384]{1,0:T(8,128)(2,1)} %bitcast.10, f32[7,384]{1,0:T(8,128)} %dynamic-slice_bitcast_fusion.taps_ref, bf16[8,128,1024]{2,1,0:T(8,128)(2,1)} %bitcast.12, f32[128]{0:T(128)} %dynamic_slice.11.skip_ref, ...), custom_call_target="tpu_custom_call" | custom-call | flops 7516192768 | bytes 4194304 | tf_op jit(solution)/shard_map/pallas_call | solution.py:262
  65.0 3.1 %copy.16 = bf16[1024,1024]{1,0:T(8,128)(2,1)} copy(bf16[1024,1024]{1,0:T(8,128)(2,1)} %bitcast.8) | data formatting | bytes 4194304
  (1 shorter events, 0.0 us)
Async XLA Ops:
  0.0 4.8 %copy-start = (bf16[3,1024,512]{2,1,0:T(8,128)(2,1)S(1)}, bf16[3,1024,512]{2,1,0:T(8,128)(2,1)}, u32[]{:S(2)}) copy-start(bf16[3,1024,512]{2,1,0:T(8,128)(2,1)} %param.14) | copy-start | bytes 9437188
where the time goes:
time: 68.3 us; the launch traced here: 68.1 us
  Pallas kernels  59.2 us (87%)
  local copies, waits for them, and re-layouts  6.76 us (10%)
  other arithmetic  2.07 us (3%)
    pallas_call x1, Pallas kernels, mix(): pl.pallas_call(functools.partial(mixer_kernel, blocks, ch_count), grid=(b...  59.2 us
    unnamed x3, local copies, waits for them, and re-layouts  3.08 us
    reduce_sum x1, other arithmetic, shards(): squares = jnp.sum(values * values, axis=0)[None, :]  2.07 us
    dynamic_slice x1, local copies, waits for them, and re-layouts, shards(): skip = lax.dynamic_slice_in_dim(skip_gain, start, group)  1.43 us

commit v1 on v0

--- a/solution.py
+++ b/solution.py
@@ -36,18 +36,19 @@
         jnp.asarray(first.T / length, bf),
         jnp.asarray(np.cos(psi), jnp.float32),
         jnp.asarray(np.sin(psi), jnp.float32),
-        jnp.asarray(second, bf),
-        jnp.asarray(second_inv, bf),
+        jnp.asarray(second, jnp.float32),
+        jnp.asarray(second_inv, jnp.float32),
     )
 
 
 def mixer_kernel(
-    seq_count, ch_count,
-    ids_ref, squares_ref, proj_ref, taps_ref, filter_ref, skip_ref,
-    t1_ref, t1i_ref, c_ref, s_ref, w2_ref, w2i_ref,
+    seq_count, ch_count, sliced,
+    ids_ref, emb_ref, proj_ref, short_ref, filter_ref, skip_ref,
+    t1_ref, t1i_ref, c_ref, s_ref, w2_wide, w2i_wide,
     out_ref,
-    ids_all, squares_all, table, feats, first, zs, filt, hs, ys, send,
-    ids_send, ids_recv, sq_send, sq_recv, filt_send, filt_recv, filt_own, out_send, out_recv, out_own,
+    w2_ref, w2i_ref,
+    ids_all, squares_ref, squares_all, proj, taps_ref, table, feats, first, zs, filt, hs, ys, send,
+    proj_sem, ids_send, ids_recv, sq_send, sq_recv, filt_send, filt_recv, filt_own, out_send, out_recv, out_own,
 ):
     me, ch = lax.axis_index("seq"), lax.axis_index("ch")
     step, steps = pl.program_id(0), pl.num_programs(0)
@@ -99,11 +100,27 @@
 
     @pl.when(step == 0)
     def _():
+        offset = 0 if sliced else pl.multiple_of(me * group, LANES)
+        loads = [
+            pltpu.make_async_copy(proj_ref.at[j, pl.ds(offset, width), :], proj.at[j], proj_sem.at[j])
+            for j in range(3)
+        ]
+        for copy in loads:
+            copy.start()
         barrier = pltpu.get_barrier_semaphore()
         for d in range(1, seq_count):
             pl.semaphore_signal(barrier, inc=1, device_id=along_seq(d), device_id_type=MESH)
         for d in range(1, ch_count):
             pl.semaphore_signal(barrier, inc=1, device_id=along_ch(d), device_id_type=MESH)
+        chunk = LANES
+
+        def add_chunk(i, total):
+            values = emb_ref[pl.ds(pl.multiple_of(i * chunk, chunk), chunk), :].astype(f32)
+            return total + jnp.sum(values * values, axis=0, keepdims=True)
+
+        squares_ref[...] = lax.fori_loop(
+            0, emb_ref.shape[0] // chunk, add_chunk, jnp.zeros((1, vocab), f32)
+        )
         pl.semaphore_wait(barrier, seq_count + ch_count - 2)
         small = [
             remote(squares_ref, squares_all.at[ch], sq_send.at[d], sq_recv.at[d], along_ch(d))
@@ -126,16 +143,21 @@
         ids_all[me] = ids_ref[...]
         squares_all[ch] = squares_ref[...]
         feats[:HISTORY] = jnp.zeros((HISTORY, 3 * width), f32)
-        for copy in small:
+        for j in range(3):
+            taps_ref[:, j * width : (j + 1) * width] = short_ref[j, :, pl.ds(offset, width)]
+        w2_ref[...] = w2_wide[...].astype(bf)
+        w2i_ref[...] = w2i_wide[...].astype(bf)
+        for copy in loads + small:
             copy.wait()
         total = squares_all[0]
         for other in range(1, ch_count):
             total = total + squares_all[other]
         scale = 1.0 / jnp.sqrt(total / MIXER_CHANNELS + EPSILON)
-        for v in range(vocab // LANES):
-            at = slice(v * LANES, (v + 1) * LANES)
-            column = jnp.broadcast_to(scale[:, at], (LANES, LANES)).T[:, :1]
-            table[at] = (proj_ref[at].astype(f32) * column).astype(bf)
+        for j in range(3):
+            for v in range(vocab // LANES):
+                at = slice(v * LANES, (v + 1) * LANES)
+                scaled = proj[j, :, at].astype(f32) * scale[:, at]
+                table[at, j * width : (j + 1) * width] = scaled.T.astype(bf)
 
     @pl.when(step < blocks)
     def _():
@@ -146,8 +168,8 @@
         lane = lax.broadcasted_iota(jnp.int32, (LANES, vocab), 1).astype(f32)
         for i in range(per):
             ids = ids_all[step, :, i * LANES : (i + 1) * LANES].astype(f32)
-            column = jnp.broadcast_to(ids, (LANES, LANES)).T[:, :1]
-            onehot = (lane == column).astype(bf)
+            column = jnp.broadcast_to(ids, (LANES, LANES)).T
+            onehot = (lane == jnp.concatenate([column] * (vocab // LANES), axis=1)).astype(bf)
             feats[HISTORY + i * LANES : HISTORY + (i + 1) * LANES] = jnp.dot(
                 onehot, table[...], preferred_element_type=f32
             )
@@ -181,9 +203,8 @@
 
         cos, sin = c_ref[...], s_ref[...]
 
-        @pl.loop(0, rows // BATCH)
-        def _(turn):
-            base = pl.multiple_of(turn * (BATCH * coarse), BATCH * coarse)
+        for turn in range(rows // BATCH):
+            base = turn * BATCH * coarse
             zbase = pl.multiple_of((g * rows + turn * BATCH) * coarse, BATCH * coarse)
             parts = []
             for i in range(BATCH):
@@ -219,7 +240,7 @@
                     t1i_ref[...], jnp.concatenate(cols, axis=1).astype(bf), preferred_element_type=f32
                 )
                 for o in range(2):
-                    skip = skip_ref[g * rows + turn * BATCH + i + o]
+                    skip = skip_ref[(0 if sliced else me * group) + g * rows + turn * BATCH + i + o]
                     z = zs[pl.ds(zbase + (i + o) * coarse, coarse), :]
                     ys[pl.ds(base + (i + o) * coarse, coarse), :] = (
                         res[:, o * LANES : (o + 1) * LANES] + skip * z
@@ -248,28 +269,36 @@
                 result_to(g, d).wait()
 
 
-def mix(ids, squares, proj, taps_rows, filt, skip, ch_count):
+def mix(ids, embedding, projected, short_taps, filt, skip, ch_count, sliced):
     blocks, group, tokens = filt.shape
     length = blocks * tokens
     coarse = length // LANES
     groups = group // GROUP
-    vocab, wide = proj.shape
+    vocab = embedding.shape[1]
+    taps = short_taps.shape[1]
+    width = -(-group // LANES) * LANES
+    wide = 3 * width
     tables = transform_tables(length)
     f32, bf = jnp.float32, jnp.bfloat16
     dma, vmem = pltpu.SemaphoreType.DMA, pltpu.VMEM
-    whole = lambda t: pl.BlockSpec(t.shape, lambda i: (0, 0))
+    whole = lambda t: pl.BlockSpec(t.shape, lambda i: (0,) * t.ndim)
     anywhere = pl.BlockSpec(memory_space=pl.ANY)
     return pl.pallas_call(
-        functools.partial(mixer_kernel, blocks, ch_count),
+        functools.partial(mixer_kernel, blocks, ch_count, sliced),
         grid=(blocks + groups,),
         out_shape=jax.ShapeDtypeStruct((blocks, group, tokens), bf),
-        in_specs=[whole(ids), whole(squares), whole(proj), whole(taps_rows), anywhere]
+        in_specs=[whole(ids), whole(embedding), anywhere, whole(short_taps), anywhere]
         + [pl.BlockSpec(memory_space=pltpu.SMEM)]
         + [whole(t) for t in tables],
         out_specs=anywhere,
         scratch_shapes=[
+            vmem((2 * LANES, 2 * LANES), bf),
+            vmem((2 * LANES, 2 * LANES), bf),
             vmem((blocks, 1, tokens), jnp.int32),
+            vmem((1, vocab), f32),
             vmem((ch_count, 1, vocab), f32),
+            vmem((3, width, vocab), bf),
+            vmem((taps, wide), f32),
             vmem((vocab, wide), bf),
             vmem((HISTORY + tokens, wide), f32),
             vmem((blocks, group, tokens), f32),
@@ -278,6 +307,7 @@
             vmem((GROUP * coarse, LANES), f32),
             vmem((GROUP * coarse, LANES), f32),
             vmem((groups, blocks, GROUP, tokens), bf),
+            dma((3,)),
             dma((blocks,)),
             dma((blocks,)),
             dma((ch_count,)),
@@ -297,35 +327,32 @@
             bytes_accessed=group * length * 4,
             transcendentals=0,
         ),
-    )(ids, squares, proj, taps_rows, filt, skip, *tables)
+    )(ids, embedding, projected, short_taps, filt, skip, *tables)
 
 
 def shards(token_ids, embedding, projected, short_taps, long_filter, skip_gain):
     seq_count = lax.axis_size("seq")
-    seq_index = lax.axis_index("seq")
-    local_ch, vocab = embedding.shape
+    local_ch = embedding.shape[0]
     tokens = token_ids.shape[0]
-    taps = short_taps.shape[0]
     group = local_ch // seq_count
-    start = seq_index * group
-
-    values = embedding.astype(jnp.float32)
-    squares = jnp.sum(values * values, axis=0)[None, :]
-    proj = lax.dynamic_slice_in_dim(projected, start, group, axis=1)
-    taps_rows = lax.dynamic_slice_in_dim(short_taps, start, group, axis=2)
-    skip = lax.dynamic_slice_in_dim(skip_gain, start, group)
-    width = -(-group // LANES) * LANES
-    if width != group:
-        proj = jnp.pad(proj, ((0, 0), (0, width - group), (0, 0)))
-        taps_rows = jnp.pad(taps_rows, ((0, 0), (0, 0), (0, width - group)))
+    sliced = group % LANES != 0
+    if sliced:
+        start = lax.axis_index("seq") * group
+        short = LANES - group % LANES
+        projected = lax.dynamic_slice_in_dim(projected, start, group, axis=1)
+        short_taps = lax.dynamic_slice_in_dim(short_taps, start, group, axis=2)
+        skip_gain = lax.dynamic_slice_in_dim(skip_gain, start, group)
+        projected = jnp.pad(projected, ((0, 0), (0, short), (0, 0)))
+        short_taps = jnp.pad(short_taps, ((0, 0), (0, 0), (0, short)))
     mixed = mix(
         token_ids[None, :],
-        squares,
-        proj.reshape(3 * width, vocab).T,
-        taps_rows.reshape(taps, 3 * width),
+        embedding,
+        projected,
+        jnp.transpose(short_taps, (1, 0, 2)),
         long_filter.reshape(seq_count, group, tokens),
-        skip,
+        skip_gain,
         lax.axis_size("ch"),
+        sliced,
     )
     return mixed.reshape(local_ch, tokens)
 

time: 68.3 us -> 62.4 us (0.914)
  local copies, waits for them, and re-layouts: 6.76 us -> 3.08 us
  other arithmetic: 2.07 us -> 0 us
    reshape x2 -> x0, local copies, waits for them, and re-layouts: 2.22 us -> none  [the longest x1 1.3 us: shards(): taps_rows.reshape(taps, 3 * width)]
    reduce_sum x1 -> x0, other arithmetic: 2.07 us -> none  [shards(): squares = jnp.sum(values * values, axis=0)[None, :]]
    dynamic_slice x2 -> x0, local copies, waits for them, and re-layouts: 1.45 us -> none  [the longest x1 1.43 us: shards(): skip = lax.dynamic_slice_in_dim(skip_gain, start, group)]
    unnamed x3 -> x1, local copies, waits for them, and re-layouts: 3.08 us -> 3.08 us
where the time goes in v1:
time: 62.4 us; the launch traced here: 62.2 us
  Pallas kernels  59.1 us (95%)
  local copies, waits for them, and re-layouts  3.08 us (5%)
    pallas_call x1, Pallas kernels, mix(): pl.pallas_call(functools.partial(mixer_kernel, blocks, ch_count, sliced),...  59.1 us
    unnamed x1, local copies, waits for them, and re-layouts  3.08 us

profile of v1, /device:TPU:0, one launch (start us, length us, event | category | flops | bytes accessed | tf_op | source)
XLA Modules:
  0.0 62.2 jit_solution(14413813307542363042)
XLA Ops:
  0.0 59.1 %shard_map.118 = bf16[8,128,1024]{2,1,0:T(8,128)(2,1)} custom-call(s32[1,1024]{1,0:T(1,128)} %bitcast.7, bf16[1024,512]{1,0:T(8,128)(2,1)} %emb_ref.1, bf16[3,1024,512]{2,1,0:T(8,128)(2,1)} %proj_ref.1, f32[3,7,1024]{2,1,0:T(8,128)} %bitcast.6, bf16[8,128,1024]{2,1,0:T(8,128)(2,1)} %bitcast.5, f32[1024]{0:T(1024)} %skip_ref.1, ...), custom_call_target="tpu_custom_call" | custom-call | flops 7516192768 | bytes 4194304 | tf_op jit(solution)/shard_map/pallas_call | solution.py:286
  59.1 3.1 %copy.14 = bf16[1024,1024]{1,0:T(8,128)(2,1)} copy(bf16[1024,1024]{1,0:T(8,128)(2,1)} %bitcast.4) | data formatting | bytes 4194304

commit v2 on v1

--- a/solution.py
+++ b/solution.py
@@ -56,6 +56,7 @@
     group = groups * rows
     per = tokens // LANES
     coarse = blocks * per
+    pitch = coarse + 1
     vocab = table.shape[0]
     width = table.shape[1] // 3
     taps = taps_ref.shape[0]
@@ -199,17 +200,17 @@
         for s in range(blocks):
             for q in range(per):
                 cols = slice(q * LANES, (q + 1) * LANES)
-                hs[pl.ds(s * per + q, rows, stride=coarse), :] = filt[g, s, :, cols].astype(f32)
+                hs[pl.ds(s * per + q, rows, stride=pitch), :] = filt[g, s, :, cols].astype(f32)
 
         cos, sin = c_ref[...], s_ref[...]
 
         for turn in range(rows // BATCH):
-            base = turn * BATCH * coarse
+            base = turn * BATCH * pitch
             zbase = pl.multiple_of((g * rows + turn * BATCH) * coarse, BATCH * coarse)
             parts = []
             for i in range(BATCH):
                 z = zs[pl.ds(zbase + i * coarse, coarse), :]
-                h = hs[pl.ds(base + i * coarse, coarse), :]
+                h = hs[base + i * pitch : base + i * pitch + coarse, :]
                 both = jnp.concatenate([z, h], axis=1).astype(bf)
                 spread = jnp.dot(t1_ref[...], both, preferred_element_type=f32)
                 for side in range(2):
@@ -242,14 +243,14 @@
                 for o in range(2):
                     skip = skip_ref[(0 if sliced else me * group) + g * rows + turn * BATCH + i + o]
                     z = zs[pl.ds(zbase + (i + o) * coarse, coarse), :]
-                    ys[pl.ds(base + (i + o) * coarse, coarse), :] = (
+                    ys[base + (i + o) * pitch : base + (i + o) * pitch + coarse, :] = (
                         res[:, o * LANES : (o + 1) * LANES] + skip * z
                     )
 
         for s in range(blocks):
             for q in range(per):
                 cols = slice(q * LANES, (q + 1) * LANES)
-                long_out = ys[pl.ds(s * per + q, rows, stride=coarse), :].astype(bf)
+                long_out = ys[pl.ds(s * per + q, rows, stride=pitch), :].astype(bf)
                 send[g, s, :, cols] = (first[s, rows_of(g), cols] * long_out.astype(f32)).astype(bf)
 
         @pl.loop(1, blocks)
@@ -304,8 +305,8 @@
             vmem((blocks, group, tokens), f32),
             vmem((group * coarse, LANES), f32),
             vmem((groups, blocks, GROUP, tokens), bf),
-            vmem((GROUP * coarse, LANES), f32),
-            vmem((GROUP * coarse, LANES), f32),
+            vmem((GROUP * (coarse + 1), LANES), f32),
+            vmem((GROUP * (coarse + 1), LANES), f32),
             vmem((groups, blocks, GROUP, tokens), bf),
             dma((3,)),
             dma((blocks,)),

time: 62.4 us -> 61.9 us (level)
  no operation moved by 1% of the time
where the time goes in v2:
time: 61.9 us; the launch traced here: 61.8 us
  Pallas kernels  58.7 us (95%)
  local copies, waits for them, and re-layouts  3.08 us (5%)
    pallas_call x1, Pallas kernels, mix(): pl.pallas_call(functools.partial(mixer_kernel, blocks, ch_count, sliced),...  58.7 us
    unnamed x1, local copies, waits for them, and re-layouts  3.08 us

profile of v2, /device:TPU:0, one launch (start us, length us, event | category | flops | bytes accessed | tf_op | source)
XLA Modules:
  0.0 61.8 jit_solution(16613760979561069227)
XLA Ops:
  0.0 58.7 %shard_map.118 = bf16[8,128,1024]{2,1,0:T(8,128)(2,1)} custom-call(s32[1,1024]{1,0:T(1,128)} %bitcast.7, bf16[1024,512]{1,0:T(8,128)(2,1)} %emb_ref.1, bf16[3,1024,512]{2,1,0:T(8,128)(2,1)} %proj_ref.1, f32[3,7,1024]{2,1,0:T(8,128)} %bitcast.6, bf16[8,128,1024]{2,1,0:T(8,128)(2,1)} %bitcast.5, f32[1024]{0:T(1024)} %skip_ref.1, ...), custom_call_target="tpu_custom_call" | custom-call | flops 7516192768 | bytes 4194304 | tf_op jit(solution)/shard_map/pallas_call | solution.py:287
  58.7 3.1 %copy.14 = bf16[1024,1024]{1,0:T(8,128)(2,1)} copy(bf16[1024,1024]{1,0:T(8,128)(2,1)} %bitcast.4) | data formatting | bytes 4194304

commit v3 on v2

--- a/solution.py
+++ b/solution.py
@@ -13,7 +13,7 @@
 EPSILON = 1e-06
 LANES = 128
 GROUP = 16
-BATCH = 8
+BATCH = 4
 HISTORY = 8
 VMEM_LIMIT = 56 * 1024 * 1024
 MESH = pl.DeviceIdType.MESH

time: 61.9 us -> 62.7 us (1.013)
  Pallas kernels: 58.7 us -> 59.5 us
    pallas_call x1, Pallas kernels: 58.7 us -> 59.5 us  [mix(): pl.pallas_call(functools.partial(mixer_kernel, blocks, ch_count, sliced),...]
where the time goes in v3:
time: 62.7 us; the launch traced here: 62.6 us
  Pallas kernels  59.5 us (95%)
  local copies, waits for them, and re-layouts  3.08 us (5%)
    pallas_call x1, Pallas kernels, mix(): pl.pallas_call(functools.partial(mixer_kernel, blocks, ch_count, sliced),...  59.5 us
    unnamed x1, local copies, waits for them, and re-layouts  3.08 us

profile of v3, /device:TPU:0, one launch (start us, length us, event | category | flops | bytes accessed | tf_op | source)
XLA Modules:
  0.0 62.6 jit_solution(11677564075427922843)
XLA Ops:
  0.0 59.5 %shard_map.118 = bf16[8,128,1024]{2,1,0:T(8,128)(2,1)} custom-call(s32[1,1024]{1,0:T(1,128)} %bitcast.7, bf16[1024,512]{1,0:T(8,128)(2,1)} %emb_ref.1, bf16[3,1024,512]{2,1,0:T(8,128)(2,1)} %proj_ref.1, f32[3,7,1024]{2,1,0:T(8,128)} %bitcast.6, bf16[8,128,1024]{2,1,0:T(8,128)(2,1)} %bitcast.5, f32[1024]{0:T(1024)} %skip_ref.1, ...), custom_call_target="tpu_custom_call" | custom-call | flops 7516192768 | bytes 4194304 | tf_op jit(solution)/shard_map/pallas_call | solution.py:287
  59.5 3.1 %copy.14 = bf16[1024,1024]{1,0:T(8,128)(2,1)} copy(bf16[1024,1024]{1,0:T(8,128)(2,1)} %bitcast.4) | data formatting | bytes 4194304
